TPU v7x, 32 devices: a whole 2x2x4 slice. The times are simulated.
32 devices in a mesh: group: 2 (over x), rep: 16 (over z, y, core).
Axes of the slice: x: 2, y: 2, z: 4, core: 2. Of those that a mesh axis runs over, the one named last changes fastest.
Arguments:
- archive: bfloat16 [1024, 32768], P('group', 'rep'), parts along dimension 0, may hold values from -6 to 6
- w_first: bfloat16 [65536, 1024], P(('group', 'rep')), parts along dimension 0, may hold values from -0.03125 to 0.03125
- b_first: float32 [2048], P('group'), parts along dimension 0, may hold values from -1 to 1
- w_second: bfloat16 [2048, 256], P('group'), parts along dimension 0, may hold values from -0.1875 to 0.1875
- pair_table: int32 [4096, 3], P(('group', 'rep')), parts along dimension 0, may hold values from 0 to 127, as said below
Outputs:
- score: float32 [2], P('group'), parts along dimension 0
- grad_first: float32 [65536, 1024], P(('group', 'rep')), parts along dimension 0
- grad_bias: float32 [2048], P('group'), parts along dimension 0
- grad_second: float32 [2048, 256], P('group'), parts along dimension 0
There are 2 independent parts, one for each index of `group`. A program takes and returns all parts, laid end to end along the dimension named above; each array names one. Nothing has to cross between parts.
Inputs may be any that keep to these rules, and one draw needn't show every extreme that they name: `pair_table`: column 1 equals column 0 plus 16; column 2 is a trajectory below 4; columns 0 and 1 are steps within that trajectory.
All inputs are finite; a program needn't handle non-finite values.
Results may differ from a plain program's by a relative error of at most 0.028.
The roundings to bfloat16 on the way count: a program that leaves them out, or rounds other values in their place, can miss the bound.
Values may be sent and summed in bfloat16 or wider, within the bound.
A program may use at most 128 MiB of HBM per device.

v0:
```python
import jax
import jax.numpy as jnp
from jax import lax
from jax.sharding import PartitionSpec as P

TRAJS = 4


EPS = 0.001
PRECISE = lax.Precision.HIGHEST


def vamp_score(sum_inst, sum_lag, cov_inst, cov_cross, cov_lag, total_pairs):
    mean_inst = sum_inst / total_pairs
    mean_lag = sum_lag / total_pairs
    identity = jnp.eye(sum_inst.shape[0], dtype=jnp.float32)
    c_inst = cov_inst / total_pairs - mean_inst[:, None] * mean_inst[None, :] + EPS * identity
    c_cross = cov_cross / total_pairs - mean_inst[:, None] * mean_lag[None, :]
    c_lag = cov_lag / total_pairs - mean_lag[:, None] * mean_lag[None, :] + EPS * identity
    chol_inst = jnp.linalg.cholesky(c_inst)
    chol_lag = jnp.linalg.cholesky(c_lag)
    whitened = jax.scipy.linalg.solve_triangular(chol_inst, c_cross, lower=True)
    koopman = jax.scipy.linalg.solve_triangular(chol_lag, whitened.T, lower=True)
    return 1.0 + jnp.sum(koopman * koopman)


def score_grads(stats, total_pairs):

    def wrapped(sum_inst, sum_lag, cov_inst, cov_cross, cov_lag):
        return vamp_score(sum_inst, sum_lag, cov_inst, cov_cross, cov_lag, total_pairs)

    value, pullback = jax.vjp(wrapped, stats[0], stats[1], stats[2], stats[3], stats[4])
    return (value, pullback(jnp.ones_like(value)))


def per_device(archive, w_first, b_first, w_second, pair_table):
    frames_total = archive.shape[0]
    steps_len = frames_total // TRAJS
    total_pairs = float(pair_table.shape[0] * lax.axis_size("rep"))
    block_rows = archive
    pre_act = (
        lax.psum_scatter(
            jnp.dot(block_rows, w_first, preferred_element_type=jnp.float32),
            "rep",
            scatter_dimension=0,
            tiled=True,
        )
        + b_first
    )
    hidden = jax.nn.elu(pre_act).astype(jnp.bfloat16)
    own_features = jnp.dot(hidden, w_second, preferred_element_type=jnp.float32).astype(
        jnp.bfloat16
    )
    features = lax.all_gather(own_features, "rep", axis=0, tiled=True)
    inst_index = pair_table[:, 2] * steps_len + pair_table[:, 0]
    lag_index = pair_table[:, 2] * steps_len + pair_table[:, 1]
    inst_rows = jnp.take(features, inst_index, axis=0)
    lag_rows = jnp.take(features, lag_index, axis=0)
    sum_inst = jnp.sum(inst_rows.astype(jnp.float32), axis=0)
    sum_lag = jnp.sum(lag_rows.astype(jnp.float32), axis=0)
    cov_inst = jnp.dot(inst_rows.T, inst_rows, preferred_element_type=jnp.float32)
    cov_cross = jnp.dot(inst_rows.T, lag_rows, preferred_element_type=jnp.float32)
    cov_lag = jnp.dot(lag_rows.T, lag_rows, preferred_element_type=jnp.float32)
    stats = lax.psum((sum_inst, sum_lag, cov_inst, cov_cross, cov_lag), "rep")
    score, grads = score_grads(stats, total_pairs)
    g_si, g_sl, g_ii, g_il, g_ll = grads
    inst_float = inst_rows.astype(jnp.float32)
    lag_float = lag_rows.astype(jnp.float32)
    d_inst = (
        g_si[None, :]
        + jnp.dot(inst_float, g_ii + g_ii.T, precision=PRECISE)
        + jnp.dot(lag_float, g_il.T, precision=PRECISE)
    )
    d_lag = (
        g_sl[None, :]
        + jnp.dot(inst_float, g_il, precision=PRECISE)
        + jnp.dot(lag_float, g_ll + g_ll.T, precision=PRECISE)
    )
    frame_terms = (
        jnp.zeros(features.shape, jnp.float32).at[inst_index].add(d_inst).at[lag_index].add(d_lag)
    )
    frame_grad = lax.psum_scatter(frame_terms, "rep", scatter_dimension=0, tiled=True).astype(
        jnp.bfloat16
    )
    slope = jnp.where(pre_act > 0, 1.0, jnp.exp(jnp.minimum(pre_act, 0.0)))
    d_pre = (jnp.dot(frame_grad, w_second.T, preferred_element_type=jnp.float32) * slope).astype(
        jnp.bfloat16
    )
    local_second = jnp.dot(hidden.T, frame_grad, preferred_element_type=jnp.float32)
    local_bias = jnp.sum(d_pre.astype(jnp.float32), axis=0)
    grad_second, grad_bias = lax.psum((local_second, local_bias), "rep")
    block_rows = archive
    grad_first = lax.dot_general(
        block_rows,
        lax.all_gather(d_pre, "rep", axis=0, tiled=True),
        (((0,), (0,)), ((), ())),
        preferred_element_type=jnp.float32,
    )
    return (score.reshape(1), grad_first, grad_bias, grad_second)


def solution(mesh):
    placed = (
        P("group", "rep"),
        P(("group", "rep"), None),
        P("group"),
        P("group", None),
        P(("group", "rep"), None),
    )
    return jax.shard_map(
        per_device,
        mesh=mesh,
        in_specs=placed,
        out_specs=(P("group"), P(("group", "rep"), None), P("group"), P("group", None)),
        check_vma=False,
    )
```

profile of v0, /device:TPU:27, one launch (start us, length us, event | category | flops | bytes accessed | tf_op | source)
XLA Modules:
  0.0 677.0 jit_solution(6192203816356908963)
XLA Ops:
  8.8 5.8 fusion.121
  16.5 58.0 %reduce-scatter.3.cloned.1.call-done = f32[32,1024]{1,0:T(8,128)} async-done(((f32[512,1024]{1,0:T(8,128)}), f32[32,1024]{1,0:T(8,128)}) %reduce-scatter.3.cloned.1.call-update) | async-done | bytes 131088 | tf_op jit(solution)/shard_map/reduce_scatter | solution.py:42
  75.6 18.8 %all_gather.6 = bf16[512,256]{1,0:T(8,128)(2,1)S(1)} all-gather(bf16[32,256]{1,0:T(8,128)(2,1)S(1)} %convolution_convert_fusion), channel_id=1, replica_groups=mesh['group'=2,'rep'=16] {'rep'}, dimensions={0}, use_global_device_ids=true | all-gather | bytes 278528 | tf_op jit(solution)/shard_map/all_gather | solution.py:54
  99.4 26.2 %all-reduce.1 = (f32[256]{0:T(256)S(1)}, f32[256]{0:T(256)S(1)}) all-reduce(f32[256]{0:T(256)S(1)} %convert_reduce_fusion.1, f32[256]{0:T(256)S(1)} %convert_reduce_fusion.2), channel_id=1, replica_groups=mesh['group'=2,'rep'=16] {'rep'}, use_global_device_ids=true, to_apply=%region_10.13 | all-reduce | flops 512 | bytes 4096 | tf_op jit(solution)/shard_map/psum | solution.py:64
  126.1 94.4 %all-reduce.8.cloned.1.call-done = (f32[256,256]{0,1:T(8,128)}, f32[256,256]{0,1:T(8,128)}, f32[256,256]{0,1:T(8,128)}) async-done(((f32[256,256]{0,1:T(8,128)}, f32[256,256]{0,1:T(8,128)}, f32[256,256]{0,1:T(8,128)}), (f32[256,256]{0,1:T(8,128)}, f32[256,256]{0,1:T(8,128)}, f32[256,256]{0,1:T(8,128)})) %all-reduce.8.cloned.1.call-update) | async-done | bytes 786448 | tf_op jit(solution)/shard_map/psum | solution.py:64
  220.5 2.0 select_add_fusion.1
  223.4 11.7 %cholesky.164 = f32[128,128]{1,0:T(8,128)S(1)} custom-call(f32[128,128]{1,0:T(8,128)S(1)} %cholesky.197), custom_call_target="Cholesky" | custom-call | tf_op jit(solution)/shard_map/jvp(jit(cholesky))/cholesky | solution.py:20
  235.2 9.8 %custom-call.28 = f32[1,128,128]{1,2,0:T(8,128)S(1)} custom-call(f32[1,128,128]{2,1,0:T(8,128)S(1)} %get-tuple-element.200), custom_call_target="InvertDiagBlocksLowerTriangular" | custom-call | tf_op jit(solution)/shard_map/jvp(jit(cholesky))/cholesky | solution.py:20
  247.2 11.7 %cholesky.181 = f32[128,128]{1,0:T(8,128)S(1)} custom-call(f32[128,128]{1,0:T(8,128)S(1)} %convolution_subtract_fusion.10), custom_call_target="Cholesky" | custom-call | tf_op jit(solution)/shard_map/jvp(jit(cholesky))/cholesky | solution.py:20
  264.2 6.6 while.22
  265.5 2.0 bitcast_dynamic-update-slice_fusion.8
  268.8 2.0 bitcast_dynamic-update-slice_fusion.8
  270.8 20.7 %custom-call.29 = f32[2,128,128]{1,2,0:T(8,128)S(1)} custom-call(f32[2,128,128]{2,1,0:T(8,128)} %get-tuple-element.111), custom_call_target="InvertDiagBlocksLowerTriangular" | custom-call | tf_op jit(solution)/shard_map/jvp(jit(_solve_triangular))/triangular_solve | solution.py:22
  297.7 11.7 %cholesky.130 = f32[128,128]{1,0:T(8,128)S(1)} custom-call(f32[128,128]{1,0:T(8,128)S(1)} %cholesky.194), custom_call_target="Cholesky" | custom-call | tf_op jit(solution)/shard_map/jvp(jit(cholesky))/cholesky | solution.py:21
  310.0 9.8 %custom-call.27 = f32[1,128,128]{1,2,0:T(8,128)S(1)} custom-call(f32[1,128,128]{2,1,0:T(8,128)S(1)} %get-tuple-element.196), custom_call_target="InvertDiagBlocksLowerTriangular" | custom-call | tf_op jit(solution)/shard_map/jvp(jit(cholesky))/cholesky | solution.py:21
  322.0 11.7 %cholesky.147 = f32[128,128]{1,0:T(8,128)S(1)} custom-call(f32[128,128]{1,0:T(8,128)S(1)} %convolution_subtract_fusion.11), custom_call_target="Cholesky" | custom-call | tf_op jit(solution)/shard_map/jvp(jit(cholesky))/cholesky | solution.py:21
  338.6 5.2 while.23
  343.9 19.9 %custom-call.30 = f32[2,128,128]{1,2,0:T(8,128)S(1)} custom-call(f32[2,128,128]{2,1,0:T(8,128)S(1)} %get-tuple-element.112), custom_call_target="InvertDiagBlocksLowerTriangular" | custom-call | tf_op jit(solution)/shard_map/jvp(jit(_solve_triangular))/triangular_solve | solution.py:23
  383.7 5.4 while.24
  389.7 20.5 %custom-call.34 = f32[2,128,128]{1,2,0:T(8,128)S(1)} custom-call(f32[2,128,128]{2,1,0:T(8,128)} %copy-done.24), custom_call_target="InvertDiagBlocksLowerTriangular" | custom-call | tf_op jit(solution)/shard_map/transpose(jvp(jit(cholesky)))/triangular_solve/custom-call.0 | solution.py:20
  422.9 5.5 while.25
  429.0 20.7 %custom-call.37 = f32[2,128,128]{1,2,0:T(8,128)S(1)} custom-call(f32[2,128,128]{2,1,0:T(8,128)} %copy-done.25), custom_call_target="InvertDiagBlocksLowerTriangular" | custom-call | tf_op jit(solution)/shard_map/transpose(jvp(jit(cholesky)))/triangular_solve/custom-call.0 | solution.py:21
  458.6 2.0 multiply_reduce_fusion
  466.6 1.9 convolution_add_fusion.1
  475.1 54.4 %reduce-scatter.5.cloned.1.call-done = f32[32,256]{1,0:T(8,128)} async-done(((f32[512,256]{1,0:T(8,128)}), f32[32,256]{1,0:T(8,128)}) %reduce-scatter.5.cloned.1.call-update) | async-done | bytes 32784 | tf_op jit(solution)/shard_map/reduce_scatter | solution.py:82
  531.2 2.1 fusion.91
  533.9 26.0 %psum.54 = f32[1024]{0:T(1024)} all-reduce(f32[1024]{0:T(1024)S(1)} %get-tuple-element.212), channel_id=1, replica_groups=mesh['group'=2,'rep'=16] {'rep'}, use_global_device_ids=true, to_apply=%region_23.29 | all-reduce | flops 1024 | bytes 8192 | tf_op jit(solution)/shard_map/psum | solution.py:91
  559.9 11.9 %all-gather.2.cloned.1.call-done = bf16[512,1024]{1,0:T(8,128)(2,1)} async-done(((bf16[32,1024]{1,0:T(8,128)(2,1)}), bf16[512,1024]{1,0:T(8,128)(2,1)}) %all-gather.2.cloned.1.call-update) | async-done | bytes 1048592 | tf_op jit(solution)/shard_map/all_gather | solution.py:95
  571.8 6.8 %convolution_bitcast_fusion = f32[2048,1024]{0,1:T(8,128)} fusion(bf16[512,1024]{1,0:T(8,128)(2,1)} %all-gather.2.cloned.1.call-done, bf16[512,2048]{1,0:T(8,128)(2,1)S(1)} %copy-done), kind=kOutput, calls=%fused_computation.12 | convolution fusion | flops 2147483648 | bytes 11534336 | tf_op jit(solution)/shard_map/dot_general | solution.py:93
  578.7 9.3 %copy.25 = f32[2048,1024]{1,0:T(8,128)} copy(f32[2048,1024]{0,1:T(8,128)} %convolution_bitcast_fusion) | data formatting | bytes 16777216
  587.9 78.7 %all-reduce.6.cloned.1.call-done = f32[1024,256]{1,0:T(8,128)} async-done(((f32[1024,256]{1,0:T(8,128)}), f32[1024,256]{1,0:T(8,128)}) %all-reduce.6.cloned.1.call-update) | async-done | bytes 1048592 | tf_op jit(solution)/shard_map/psum | solution.py:91
  666.7 2.3 copy.89
  (195 shorter events, 104.9 us)
Async XLA Ops:
  7.2 1.6 copy-start
  7.2 67.3 %reduce-scatter.3.cloned.1.call-start = ((), (), s32[]{:S(2)}) async-start(), calls=%async_computation.2 | async-start | bytes 2228224 | tf_op jit(solution)/shard_map/reduce_scatter | solution.py:42
  14.6 1.2 copy-start.30
  14.6 59.9 %copy-start.2 = (bf16[1024,256]{1,0:T(8,128)(2,1)S(1)}, bf16[1024,256]{1,0:T(8,128)(2,1)}, u32[]{:S(2)}) copy-start(bf16[1024,256]{1,0:T(8,128)(2,1)} %param.22) | copy-start | bytes 1572868
  14.6 59.9 %copy-start.26 = (f32[1024]{0:T(1024)S(1)}, f32[1024]{0:T(1024)}, u32[]{:S(2)}) copy-start(f32[1024]{0:T(1024)} %param.21) | copy-start | bytes 12292
  14.6 205.9 %all-reduce.8.cloned.1.call-start = ((), (), s32[]{:S(2)}) async-start(), calls=%async_computation.6 | async-start | bytes 1572864 | tf_op jit(solution)/shard_map/psum | solution.py:64
  16.4 109.6 %copy-start.27 = (pred[128]{0:T(512)(128)(4,1)}, pred[128]{0:T(512)(128)(4,1)S(1)}, u32[]{:S(2)}) copy-start(pred[128]{0:T(512)(128)(4,1)S(1)} %get-tuple-element.216) | copy-start | bytes 388
  125.6 404.0 %reduce-scatter.5.cloned.1.call-start = ((), (), s32[]{:S(2)}) async-start(), calls=%async_computation.3 | async-start | bytes 557056 | tf_op jit(solution)/shard_map/reduce_scatter | solution.py:82
  222.7 0.7 copy-start.20
  259.6 11.2 %copy-start.17 = (f32[256,256]{1,0:T(8,128)}, f32[256,256]{1,0:T(8,128)S(1)}, u32[]{:S(2)}) copy-start(f32[256,256]{1,0:T(8,128)S(1)} %get-tuple-element.198) | copy-start | bytes 786436
  291.4 43.6 %copy-start.7 = (f32[2,128,128]{1,2,0:T(8,128)}, f32[2,128,128]{1,2,0:T(8,128)S(1)}, u32[]{:S(2)}) copy-start(f32[2,128,128]{1,2,0:T(8,128)S(1)} %custom-call.29) | copy-start | bytes 393220
  292.7 1.7 copy-start.3
  294.4 0.7 copy-start.12
  297.0 0.7 copy-start.21
  335.0 1.9 copy-start.19
  363.8 1.3 copy-start.9
  369.3 1.4 copy-start.4
  371.4 0.7 copy-start.16
  375.5 6.0 copy-start.8
  375.5 6.9 %copy-start.18 = (f32[256,256]{1,0:T(8,128)S(1)}, f32[256,256]{1,0:T(8,128)}, u32[]{:S(2)}) copy-start(f32[256,256]{1,0:T(8,128)} %copy-done.17) | copy-start | bytes 786436
  379.7 3.9 copy-start.5
  383.6 35.1 %copy-start.10 = (f32[2,128,128]{1,2,0:T(8,128)S(1)}, f32[2,128,128]{1,2,0:T(8,128)}, u32[]{:S(2)}) copy-start(f32[2,128,128]{1,2,0:T(8,128)} %copy-done.9) | copy-start | bytes 393220
  389.0 0.7 copy-start.24
  410.2 2.5 copy-start.22
  416.2 6.7 copy-start.6
  422.8 26.9 %copy-start.23 = (f32[256,256]{1,0:T(8,128)}, f32[256,256]{1,0:T(8,128)S(1)}, u32[]{:S(2)}) copy-start(f32[256,256]{1,0:T(8,128)S(1)} %fusion.1) | copy-start | bytes 786436
  460.6 5.3 copy-start.28
  460.6 5.3 copy-start.29
  469.6 59.9 %copy-start.11 = (f32[32,1024]{1,0:T(8,128)S(1)}, f32[32,1024]{1,0:T(8,128)}, u32[]{:S(2)}) copy-start(f32[32,1024]{1,0:T(8,128)} %reduce-scatter.3.cloned.1.call-done) | copy-start | bytes 393220
  474.2 0.8 copy-start.1
  475.1 96.8 %all-gather.2.cloned.1.call-start = ((), (), s32[]{:S(2)}) async-start(), calls=%async_computation.4 | async-start | bytes 1114112 | tf_op jit(solution)/shard_map/all_gather | solution.py:95
  531.2 135.5 %all-reduce.6.cloned.1.call-start = ((), (), s32[]{:S(2)}) async-start(), calls=%async_computation.5 | async-start | bytes 2097152 | tf_op jit(solution)/shard_map/psum | solution.py:91
  (4 other events, 2.6 us)
Sparse Core Ops, SparseCore 0:
  14.7 59.7 reduce-scatter.2
  125.7 94.7 all-reduce.7
  475.2 54.2 reduce-scatter.4
  532.3 39.4 all-gather.1
  576.1 90.4 all-reduce.5
where the time goes:
time: 687 us; the launch traced here: 677 us
  waiting for transfers between devices  298 us (43%)
  other arithmetic  172 us (25%)
  blocking collectives  71 us (10%)
  matrix products  61.9 us (9%)
  local copies, waits for them, and re-layouts  54.5 us (8%)
  between operations  19.2 us (3%)
    psum x1, waiting for transfers between devices, per_device(): stats = lax.psum((sum_inst, sum_lag, cov_inst, cov_cross, cov_lag), 'rep')  94.4 us
    psum x1, waiting for transfers between devices, per_device(): grad_second, grad_bias = lax.psum((local_second, local_bias), 'rep')  78.7 us
    reduce_scatter x1, waiting for transfers between devices, per_device(): lax.psum_scatter(jnp.dot(block_rows, w_first, preferred_element_type=jnp....  58 us
    another operation x9, other arithmetic, vamp_score(): chol_lag = jnp.linalg.cholesky(c_lag)  56.5 us
    another operation x9, other arithmetic, vamp_score(): chol_inst = jnp.linalg.cholesky(c_inst)  55.8 us
    reduce_scatter x1, waiting for transfers between devices, per_device(): lax.psum_scatter(frame_terms, 'rep', scatter_dimension=0, tiled=True)  54.4 us
    psum x1, blocking collectives, per_device(): stats = lax.psum((sum_inst, sum_lag, cov_inst, cov_cross, cov_lag), 'rep')  26.2 us
    psum x1, blocking collectives, per_device(): grad_second, grad_bias = lax.psum((local_second, local_bias), 'rep')  26 us
  transfers between devices with their start and end apart: 5, of which 5 were waited for; matrix products, arithmetic and copies ran while one was open for 3% of the time, Pallas kernels for 0%

commit v1 on v0

v1 whole, which is shorter than its diff:
```python
import functools

import jax
import jax.numpy as jnp
from jax import lax
from jax.experimental import pallas as pl
from jax.experimental.pallas import tpu as pltpu
from jax.sharding import PartitionSpec as P

TRAJS = 4
LAG_PARTS = 32
EPS = 0.001
HIGHEST = lax.Precision.HIGHEST
MIB = 1 << 20


def elu(v):
    return jnp.where(v > 0, v, jnp.exp(jnp.minimum(v, 0.0)) - 1.0)


def exchange_kernel(
    n,
    archive,
    w_first,
    b_first,
    w_second,
    count,
    feats,
    pre_all,
    count_out,
    out_half,
    in_half,
    own_half,
    send_buf,
    recv_buf,
    count_in,
    count_all,
    pair_send,
    pair_recv,
    sum_send,
    sum_recv,
    cnt_send,
    cnt_recv,
    feat_send,
    feat_recv,
    pre_send,
    pre_recv,
):
    frames, hid = archive.shape[0], w_first.shape[1]
    half = frames // 2
    chips = n // 2
    rows = frames // n
    me = lax.axis_index("rep")
    core = lax.rem(me, 2)
    chip = me // 2
    partner = me + 1 - 2 * core

    def to(device):
        return {"rep": device}

    def peer_of(d):
        other = lax.rem(chip + d, chips)
        return other, other * 2 + core

    barrier = pltpu.get_barrier_semaphore()
    pl.semaphore_signal(barrier, inc=1, device_id=to(partner), device_id_type=pl.DeviceIdType.MESH)

    @pl.loop(1, chips)
    def _(d):
        pl.semaphore_signal(
            barrier, inc=1, device_id=to(peer_of(d)[1]), device_id_type=pl.DeviceIdType.MESH
        )

    def remote(src, dst, send, recv, device):
        return pltpu.make_async_remote_copy(
            src_ref=src,
            dst_ref=dst,
            send_sem=send,
            recv_sem=recv,
            device_id=to(device),
            device_id_type=pl.DeviceIdType.MESH,
        )

    tile = 256

    def matmul(row0, nrows, dst, dst0):
        @pl.loop(0, hid // tile)
        def _(t):
            cols = pl.ds(pl.multiple_of(t * tile, tile), tile)
            dst[pl.ds(dst0, nrows), cols] = jnp.dot(
                archive[pl.ds(pl.multiple_of(row0, 32), nrows), :],
                w_first[:, cols],
                preferred_element_type=jnp.float32,
            )

    piece = half // 2
    pieces = []
    for i in range(2):
        matmul((1 - core) * half + i * piece, piece, out_half, i * piece)
        if i == 0:
            pl.semaphore_wait(barrier, chips)
            cnt_copy = remote(count, count_in, cnt_send.at[chips], cnt_recv.at[chips], partner)
            cnt_copy.start()
        part = pl.ds(i * piece, piece)
        copy = remote(out_half.at[part], in_half.at[part], pair_send.at[i], pair_recv.at[i], partner)
        copy.start()
        pieces.append(copy)
    matmul(core * half, half, own_half, 0)

    cnt_copy.wait()
    count_all[chip] = count[...] + count_in[...]

    def cnt_remote(d):
        return remote(
            count_all.at[chip], count_all.at[chip], cnt_send.at[d], cnt_recv.at[chip], peer_of(d)[1]
        )

    @pl.loop(1, chips)
    def _(d):
        cnt_remote(d).start()

    for copy in pieces:
        copy.wait()

    def sum_remote(d):
        other, device = peer_of(d)
        return remote(
            send_buf.at[other], recv_buf.at[chip], sum_send.at[d], sum_recv.at[chip], device
        )

    @pl.loop(1, chips)
    def _(d):
        other = peer_of(d)[0]
        block = pl.ds(pl.multiple_of(other * rows, rows), rows)
        send_buf[other] = (own_half[block, :] + in_half[block, :]).astype(jnp.bfloat16)
        sum_remote(d).start()

    mine = pl.ds(pl.multiple_of(chip * rows, rows), rows)
    own_half[mine, :] = own_half[mine, :] + in_half[mine, :] + b_first[...]

    @pl.loop(1, chips)
    def _(d):
        other = peer_of(d)[0]
        remote(send_buf.at[other], recv_buf.at[other], sum_send.at[d], sum_recv.at[other], partner).wait_recv()
        own_half[mine, :] = own_half[mine, :] + recv_buf[other].astype(jnp.float32)

    pre_act = own_half[mine, :]
    hidden = elu(pre_act).astype(jnp.bfloat16)
    place = pl.ds(pl.multiple_of(core * half + chip * rows, rows), rows)
    feats[place, :] = jnp.dot(hidden, w_second[...], preferred_element_type=jnp.float32).astype(
        jnp.bfloat16
    )

    def gather_remote(buf, send, recv, d):
        return remote(buf.at[place], buf.at[place], send.at[d], recv.at[chip], peer_of(d)[1])

    @pl.loop(1, chips)
    def _(d):
        gather_remote(feats, feat_send, feat_recv, d).start()

    pre_all[place, :] = pre_act.astype(jnp.bfloat16)

    @pl.loop(1, chips)
    def _(d):
        gather_remote(pre_all, pre_send, pre_recv, d).start()

    def forward(buf, send, recv):
        @pl.loop(1, chips)
        def _(d):
            other = peer_of(d)[0]
            theirs = pl.ds(pl.multiple_of(core * half + other * rows, rows), rows)
            remote(buf.at[theirs], buf.at[theirs], send.at[d], recv.at[other], partner).wait_recv()

        side = pl.ds(pl.multiple_of(core * half, half), half)
        copy = remote(buf.at[side], buf.at[side], send.at[chips], recv.at[chips], partner)
        copy.start()
        return copy

    feat_copy = forward(feats, feat_send, feat_recv)

    @pl.loop(1, chips)
    def _(d):
        other = peer_of(d)[0]
        remote(count_all.at[other], count_all.at[other], cnt_send.at[d], cnt_recv.at[other], partner).wait_recv()

    count_out[...] = jnp.sum(count_all[...], axis=0)
    pre_copy = forward(pre_all, pre_send, pre_recv)
    feat_copy.wait()
    pre_copy.wait()

    @pl.loop(1, chips)
    def _(d):
        cnt_remote(d).wait_send()
        sum_remote(d).wait_send()
        gather_remote(feats, feat_send, feat_recv, d).wait_send()
        gather_remote(pre_all, pre_send, pre_recv, d).wait_send()


def exchange(n, archive, w_first, b_first, w_second, count):
    frames, hid, feat = archive.shape[0], w_first.shape[1], w_second.shape[1]
    half, chips, rows = frames // 2, n // 2, frames // n
    vmem = pl.BlockSpec(memory_space=pltpu.VMEM)
    dma = pltpu.SemaphoreType.DMA
    return pl.pallas_call(
        functools.partial(exchange_kernel, n),
        out_shape=(
            jax.ShapeDtypeStruct((frames, feat), jnp.bfloat16),
            jax.ShapeDtypeStruct((frames, hid), jnp.bfloat16),
            jax.ShapeDtypeStruct(count.shape, jnp.float32),
        ),
        in_specs=[vmem] * 5,
        out_specs=(vmem, vmem, vmem),
        scratch_shapes=[
            pltpu.VMEM((half, hid), jnp.float32),
            pltpu.VMEM((half, hid), jnp.float32),
            pltpu.VMEM((half, hid), jnp.float32),
            pltpu.VMEM((chips, rows, hid), jnp.bfloat16),
            pltpu.VMEM((chips, rows, hid), jnp.bfloat16),
            pltpu.VMEM(count.shape, jnp.float32),
            pltpu.VMEM((chips,) + count.shape, jnp.float32),
            dma((2,)),
            dma((2,)),
            dma((chips,)),
            dma((chips,)),
            dma((chips + 1,)),
            dma((chips + 1,)),
            dma((chips + 1,)),
            dma((chips + 1,)),
            dma((chips + 1,)),
            dma((chips + 1,)),
        ],
        compiler_params=pltpu.CompilerParams(
            collective_id=0, has_side_effects=True, vmem_limit_bytes=52 * MIB
        ),
        name="exchange",
    )(archive, w_first, b_first, w_second, count)


def mm(a, b, dims=((1,), (0,))):
    return lax.dot_general(
        a, b, (dims, ((), ())), precision=HIGHEST, preferred_element_type=jnp.float32
    )


TN = ((0,), (0,))
NT = ((1,), (1,))


def score_kernel(tau, total_pairs, feats, count, score, frame_grad):
    frames, feat = feats.shape
    columns = jnp.concatenate(
        [count[...], jnp.zeros((128 - count.shape[0], 128), jnp.float32)], axis=0
    ).T
    n = jnp.concatenate([columns[:, i : i + 1] for i in range(frames // 128)], axis=0)
    first = feats[...].astype(jnp.float32)
    later = jnp.concatenate([first[tau:], first[:tau]], axis=0)
    scale = 1.0 / total_pairs
    x0 = first - jnp.sum(first * n, axis=0, keepdims=True) * scale
    xt = later - jnp.sum(later * n, axis=0, keepdims=True) * scale
    n = n * scale
    x0n = x0 * n
    xtn = xt * n
    eye = (
        lax.broadcasted_iota(jnp.int32, (feat, feat), 0)
        == lax.broadcasted_iota(jnp.int32, (feat, feat), 1)
    ).astype(jnp.float32)
    c00 = mm(x0n, x0, TN) + EPS * eye
    ctt = mm(xtn, xt, TN) + EPS * eye
    c0t = mm(x0n, xt, TN)
    top0 = jnp.max(jnp.sum(jnp.abs(c00), axis=0, keepdims=True), axis=1, keepdims=True)
    topt = jnp.max(jnp.sum(jnp.abs(ctt), axis=0, keepdims=True), axis=1, keepdims=True)
    c00 = c00 / top0
    ctt = ctt / topt
    low = EPS / jnp.max(jnp.maximum(top0, topt))

    def gain(low):
        return 4.0 / jnp.square(1.0 + low)

    a = gain(low) * ((1.0 + low) * eye - c00)
    b = gain(low) * ((1.0 + low) * eye - ctt)

    def step(carry):
        low, a, b = carry
        g = gain(low)
        s = 1.0 + low
        ra = s * eye - mm(c00, a)
        rb = s * eye - mm(ctt, b)
        return (jnp.minimum(g * low, 1.0), g * mm(a, ra), g * mm(b, rb))

    _, a, b = lax.while_loop(lambda carry: carry[0] < 1.0 - 2e-6, step, (gain(low) * low, a, b))
    a = a / top0
    b = b / topt
    u = mm(a, c0t)
    v = mm(c0t, b)
    k = mm(u, b)
    score[...] = jnp.broadcast_to(1.0 + jnp.sum(u * v), score.shape)
    g00 = -2.0 * mm(k, u, NT)
    gtt = -2.0 * mm(k, v, TN)
    k = 2.0 * k
    d0 = n * (mm(x0, g00) + mm(xt, k, NT))
    dt = n * (mm(x0, k) + mm(xt, gtt))
    dt = jnp.concatenate([dt[frames - tau :], dt[: frames - tau]], axis=0)
    frame_grad[...] = (d0 + dt).astype(jnp.bfloat16)


def score_and_grad(tau, total_pairs, feats, count):
    vmem = pl.BlockSpec(memory_space=pltpu.VMEM)
    return pl.pallas_call(
        functools.partial(score_kernel, tau, total_pairs),
        out_shape=(
            jax.ShapeDtypeStruct((8, 128), jnp.float32),
            jax.ShapeDtypeStruct(feats.shape, jnp.bfloat16),
        ),
        in_specs=[vmem] * 2,
        out_specs=(vmem, vmem),
        compiler_params=pltpu.CompilerParams(vmem_limit_bytes=52 * MIB),
        name="score",
    )(feats, count)


def per_device(n, archive, w_first, b_first, w_second, pair_table):
    frames_total = archive.shape[0]
    steps_len = frames_total // TRAJS
    tau = frames_total // LAG_PARTS
    total_pairs = float(pair_table.shape[0] * n)
    inst_index = pair_table[:, 2] * steps_len + pair_table[:, 0]
    count_rows = max(8, frames_total // 128)
    frame_ids = lax.broadcasted_iota(jnp.int32, (count_rows, 128), 0) * 128 + lax.broadcasted_iota(
        jnp.int32, (count_rows, 128), 1
    )
    count = jnp.sum(
        (inst_index[:, None, None] == frame_ids[None]).astype(jnp.float32), axis=0
    )
    feats, pre_act, count = exchange(n, archive, w_first, b_first[None, :], w_second, count)
    score, frame_grad = score_and_grad(tau, total_pairs, feats, count)
    pre_act = pre_act.astype(jnp.float32)
    hidden = elu(pre_act).astype(jnp.bfloat16)
    slope = jnp.where(pre_act > 0, 1.0, jnp.exp(jnp.minimum(pre_act, 0.0)))
    d_pre = (jnp.dot(frame_grad, w_second.T, preferred_element_type=jnp.float32) * slope).astype(
        jnp.bfloat16
    )
    grad_second = jnp.dot(hidden.T, frame_grad, preferred_element_type=jnp.float32)
    grad_bias = jnp.sum(d_pre.astype(jnp.float32), axis=0)
    grad_first = lax.dot_general(
        archive, d_pre, (((0,), (0,)), ((), ())), preferred_element_type=jnp.float32
    )
    return (score[0, :1], grad_first, grad_bias, grad_second)


def solution(mesh):
    placed = (
        P("group", "rep"),
        P(("group", "rep"), None),
        P("group"),
        P("group", None),
        P(("group", "rep"), None),
    )
    return jax.shard_map(
        functools.partial(per_device, mesh.shape["rep"]),
        mesh=mesh,
        in_specs=placed,
        out_specs=(P("group"), P(("group", "rep"), None), P("group"), P("group", None)),
        check_vma=False,
    )
```

time: 687 us -> 83.1 us (0.12); the launches traced: 677 us -> 82.7 us
  waiting for transfers between devices: 298 us -> 0 us
  other arithmetic: 172 us -> 1.04 us
  blocking collectives: 71 us -> 0 us
  Pallas kernels: 0 us -> 60.6 us
  matrix products: 61.9 us -> 8.69 us
  local copies, waits for them, and re-layouts: 54.5 us -> 11.7 us
  between operations: 19.2 us -> 0.67 us
    psum x2 -> x0, waiting for transfers between devices: 173 us -> none  [the longest x1 94.4 us: per_device(): stats = lax.psum((sum_inst, sum_lag, cov_inst, cov_cross, cov_lag), 'rep')]
    another operation x23 -> x0, other arithmetic: 156 us -> none  [the longest x9 56.5 us: vamp_score(): chol_lag = jnp.linalg.cholesky(c_lag)]
    reduce_scatter x2 -> x0, waiting for transfers between devices: 112 us -> none  [the longest x1 58 us: per_device(): lax.psum_scatter(jnp.dot(block_rows, w_first, preferred_element_type=jnp....]
    pallas_call x0 -> x2, Pallas kernels: none -> 60.6 us  [the longest x1 41.4 us: exchange(): pl.pallas_call(functools.partial(exchange_kernel, n), out_shape=(jax.Shap...]
    psum x2 -> x0, blocking collectives: 52.2 us -> none  [the longest x1 26.2 us: per_device(): stats = lax.psum((sum_inst, sum_lag, cov_inst, cov_cross, cov_lag), 'rep')]
    another operation x34 -> x0, matrix products: 29.9 us -> none  [the longest x9 8.85 us: vamp_score(): jax.scipy.linalg.solve_triangular(chol_lag, whitened.T, lower=True)]
    another operation x36 -> x0, local copies, waits for them, and re-layouts: 28.8 us -> none  [the longest x7 8.24 us: vamp_score(): whitened = jax.scipy.linalg.solve_triangular(chol_inst, c_cross, lower=True)]
    dot_general x14 -> x1, matrix products: 28.3 us -> 5.61 us  [per_device(): lax.dot_general(archive, d_pre, (((0,), (0,)), ((), ())), preferred_eleme...]
  transfers between devices with their start and end apart: 5 -> 0, of which waited for: 5 -> 0; matrix products, arithmetic and copies ran while one was open for 3% -> 0% of each run, Pallas kernels for 0% -> 0%
where the time goes in v1:
time: 83.1 us; the launch traced here: 82.7 us
  Pallas kernels  60.6 us (73%)
  local copies, waits for them, and re-layouts  11.7 us (14%)
  matrix products  8.69 us (10%)
  other arithmetic  1.04 us (1%)
    pallas_call x1, Pallas kernels, exchange(): pl.pallas_call(functools.partial(exchange_kernel, n), out_shape=(jax.Shap...  41.4 us
    pallas_call x1, Pallas kernels, score_and_grad(): pl.pallas_call(functools.partial(score_kernel, tau, total_pairs), out_sha...  19.3 us
    unnamed x9, local copies, waits for them, and re-layouts  11.2 us
    dot_general x1, matrix products, per_device(): lax.dot_general(archive, d_pre, (((0,), (0,)), ((), ())), preferred_eleme...  5.61 us
    dot_general x1, matrix products, per_device(): jnp.dot(hidden.T, frame_grad, preferred_element_type=jnp.float32)  1.69 us

profile of v1, /device:TPU:27, one launch (start us, length us, event | category | flops | bytes accessed | tf_op | source)
XLA Modules:
  0.0 82.7 jit_solution(10270841285548407889)
XLA Ops:
  0.6 0.8 add_bitcast_fusion
  1.4 0.1 iota_add_fusion
  1.5 0.2 convert_reduce_fusion.1.count
  1.7 0.0 copy-start
  1.7 1.0 %copy-done = bf16[1024,256]{1,0:T(8,128)(2,1)S(1)} copy-done((bf16[1024,256]{1,0:T(8,128)(2,1)S(1)}, bf16[1024,256]{1,0:T(8,128)(2,1)}, u32[]{:S(2)}) %copy-start) | copy-done | bytes 524312
  2.7 0.0 copy-start.2
  2.7 0.7 copy-done.2
  3.4 41.4 %exchange.1 = (bf16[512,256]{1,0:T(8,128)(2,1)S(1)}, bf16[512,1024]{1,0:T(8,128)(2,1)S(1)}, f32[8,128]{1,0:T(8,128)S(1)}) custom-call(bf16[512,2048]{1,0:T(8,128)(2,1)} %archive.1, bf16[2048,1024]{1,0:T(8,128)(2,1)} %w_first.1, f32[1,1024]{1,0:T(1,128)S(1)} %bitcast.11, bf16[1024,256]{1,0:T(8,128)(2,1)S(1)} %copy-done, f32[8,128]{1,0:T(8,128)S(1)} %convert_reduce_fusion.1.count), custom_call_target="tpu_custom_call" | custom-call | tf_op jit(solution)/shard_map/exchange/pallas_call | solution.py:204
  44.8 19.3 %score.1 = (f32[8,128]{1,0:T(8,128)S(1)}, bf16[512,256]{1,0:T(8,128)(2,1)S(1)}) custom-call(bf16[512,256]{1,0:T(8,128)(2,1)S(1)} %get-tuple-element.9.feats, f32[8,128]{1,0:T(8,128)S(1)} %get-tuple-element.10.count), custom_call_target="tpu_custom_call" | custom-call | tf_op jit(solution)/shard_map/score/pallas_call | solution.py:308
  64.1 0.5 slice.11
  64.6 0.0 copy-start.1
  64.6 1.7 %fusion.6 = f32[1024,256]{1,0:T(8,128)} fusion(bf16[512,256]{1,0:T(8,128)(2,1)S(1)} %get-tuple-element.12, bf16[512,1024]{1,0:T(8,128)(2,1)S(1)} %get-tuple-element.13), kind=kOutput, calls=%fused_computation.11 | convolution fusion | flops 271581184 | bytes 2359296 | tf_op jit(solution)/shard_map/dot_general | solution.py:342
  66.3 0.0 copy-done.1
  66.3 0.0 copy-start.3
  66.3 1.4 %convert_reduce_fusion = (f32[1024]{0:T(1024)}, bf16[512,1024]{1,0:T(8,128)(2,1)S(1)}) fusion(bf16[512,1024]{1,0:T(8,128)(2,1)S(1)} %get-tuple-element.13, bf16[512,256]{1,0:T(8,128)(2,1)S(1)} %get-tuple-element.12, bf16[1024,256]{1,0:T(8,128)(2,1)S(1)} %copy-done.1), kind=kOutput, calls=%fused_computation.10 | convolution fusion | flops 272628736 | bytes 2887680 | tf_op jit(solution)/shard_map/dot_general | solution.py:339
  67.7 0.2 copy-done.3
  67.9 5.6 %convolution_bitcast_fusion = f32[2048,1024]{0,1:T(8,128)} fusion(bf16[512,1024]{1,0:T(8,128)(2,1)S(1)} %get-tuple-element.23, bf16[512,2048]{1,0:T(8,128)(2,1)S(1)} %copy-done.3), kind=kOutput, calls=%fused_computation | convolution fusion | flops 2147483648 | bytes 11534336 | tf_op jit(solution)/shard_map/dot_general | solution.py:344
  73.5 9.2 %copy.10 = f32[2048,1024]{1,0:T(8,128)} copy(f32[2048,1024]{0,1:T(8,128)} %convolution_bitcast_fusion) | data formatting | bytes 16777216
  (1 shorter events, 0.0 us)
Async XLA Ops:
  1.7 1.0 %copy-start = (bf16[1024,256]{1,0:T(8,128)(2,1)S(1)}, bf16[1024,256]{1,0:T(8,128)(2,1)}, u32[]{:S(2)}) copy-start(bf16[1024,256]{1,0:T(8,128)(2,1)} %w_second.1) | copy-start | bytes 1572868
  2.7 0.7 copy-start.2
  64.6 1.7 %copy-start.1 = (bf16[1024,256]{1,0:T(8,128)(2,1)S(1)}, bf16[1024,256]{1,0:T(8,128)(2,1)}, u32[]{:S(2)}) copy-start(bf16[1024,256]{1,0:T(8,128)(2,1)} %w_second.1) | copy-start | bytes 1572868
  66.3 1.6 %copy-start.3 = (bf16[512,2048]{1,0:T(8,128)(2,1)S(1)}, bf16[512,2048]{1,0:T(8,128)(2,1)}, u32[]{:S(2)}) copy-start(bf16[512,2048]{1,0:T(8,128)(2,1)} %archive.1) | copy-start | bytes 6291460

commit v2 on v1

--- a/solution.py
+++ b/solution.py
@@ -10,7 +10,6 @@
 TRAJS = 4
 LAG_PARTS = 32
 EPS = 0.001
-HIGHEST = lax.Precision.HIGHEST
 MIB = 1 << 20
 
 
@@ -94,18 +93,56 @@
             )
 
     piece = half // 2
-    pieces = []
-    for i in range(2):
-        matmul((1 - core) * half + i * piece, piece, out_half, i * piece)
-        if i == 0:
+    side_chips = chips // 2
+    side = chip // side_chips
+
+    def sum_remote(other):
+        return remote(
+            send_buf.at[other],
+            recv_buf.at[chip],
+            sum_send.at[other],
+            sum_recv.at[chip],
+            other * 2 + core,
+        )
+
+    def send_sum(other):
+        block = pl.ds(pl.multiple_of(other * rows, rows), rows)
+        send_buf[other] = (own_half[block, :] + in_half[block, :]).astype(jnp.bfloat16)
+        sum_remote(other).start()
+
+    def partner_piece(which, index):
+        start = pl.multiple_of(which * piece, 32)
+        matmul((1 - core) * half + start, piece, out_half, start)
+        if index == 0:
             pl.semaphore_wait(barrier, chips)
-            cnt_copy = remote(count, count_in, cnt_send.at[chips], cnt_recv.at[chips], partner)
-            cnt_copy.start()
-        part = pl.ds(i * piece, piece)
-        copy = remote(out_half.at[part], in_half.at[part], pair_send.at[i], pair_recv.at[i], partner)
+        part = pl.ds(start, piece)
+        copy = remote(
+            out_half.at[part], in_half.at[part], pair_send.at[index], pair_recv.at[index], partner
+        )
         copy.start()
-        pieces.append(copy)
-    matmul(core * half, half, own_half, 0)
+        return copy
+
+    def own_piece(which):
+        start = pl.multiple_of(which * piece, 32)
+        matmul(core * half + start, piece, own_half, start)
+
+    far_copy = partner_piece(1 - side, 0)
+    own_piece(1 - side)
+    near_copy = partner_piece(side, 1)
+    far_copy.wait_recv()
+
+    @pl.loop(0, side_chips)
+    def _(j):
+        send_sum((1 - side) * side_chips + lax.rem(chip + j, side_chips))
+
+    cnt_copy = remote(count, count_in, cnt_send.at[chips], cnt_recv.at[chips], partner)
+    cnt_copy.start()
+    own_piece(side)
+    near_copy.wait_recv()
+
+    @pl.loop(1, side_chips)
+    def _(j):
+        send_sum(side * side_chips + lax.rem(chip + j, side_chips))
 
     cnt_copy.wait()
     count_all[chip] = count[...] + count_in[...]
@@ -119,21 +156,8 @@
     def _(d):
         cnt_remote(d).start()
 
-    for copy in pieces:
-        copy.wait()
-
-    def sum_remote(d):
-        other, device = peer_of(d)
-        return remote(
-            send_buf.at[other], recv_buf.at[chip], sum_send.at[d], sum_recv.at[chip], device
-        )
-
-    @pl.loop(1, chips)
-    def _(d):
-        other = peer_of(d)[0]
-        block = pl.ds(pl.multiple_of(other * rows, rows), rows)
-        send_buf[other] = (own_half[block, :] + in_half[block, :]).astype(jnp.bfloat16)
-        sum_remote(d).start()
+    far_copy.wait_send()
+    near_copy.wait_send()
 
     mine = pl.ds(pl.multiple_of(chip * rows, rows), rows)
     own_half[mine, :] = own_half[mine, :] + in_half[mine, :] + b_first[...]
@@ -141,7 +165,7 @@
     @pl.loop(1, chips)
     def _(d):
         other = peer_of(d)[0]
-        remote(send_buf.at[other], recv_buf.at[other], sum_send.at[d], sum_recv.at[other], partner).wait_recv()
+        remote(send_buf.at[other], recv_buf.at[other], sum_send.at[other], sum_recv.at[other], partner).wait_recv()
         own_half[mine, :] = own_half[mine, :] + recv_buf[other].astype(jnp.float32)
 
     pre_act = own_half[mine, :]
@@ -191,7 +215,7 @@
     @pl.loop(1, chips)
     def _(d):
         cnt_remote(d).wait_send()
-        sum_remote(d).wait_send()
+        sum_remote(peer_of(d)[0]).wait_send()
         gather_remote(feats, feat_send, feat_recv, d).wait_send()
         gather_remote(pre_all, pre_send, pre_recv, d).wait_send()
 
@@ -237,16 +261,21 @@
 
 
 def mm(a, b, dims=((1,), (0,))):
-    return lax.dot_general(
-        a, b, (dims, ((), ())), precision=HIGHEST, preferred_element_type=jnp.float32
-    )
+    a_top, b_top = a.astype(jnp.bfloat16), b.astype(jnp.bfloat16)
+    a_rest = (a - a_top.astype(jnp.float32)).astype(jnp.bfloat16)
+    b_rest = (b - b_top.astype(jnp.float32)).astype(jnp.bfloat16)
+
+    def dot(x, y):
+        return lax.dot_general(x, y, (dims, ((), ())), preferred_element_type=jnp.float32)
+
+    return dot(a_top, b_top) + (dot(a_top, b_rest) + dot(a_rest, b_top))
 
 
 TN = ((0,), (0,))
 NT = ((1,), (1,))
 
 
-def score_kernel(tau, total_pairs, feats, count, score, frame_grad):
+def score_into(tau, total_pairs, feats, count, score, frame_grad):
     frames, feat = feats.shape
     columns = jnp.concatenate(
         [count[...], jnp.zeros((128 - count.shape[0], 128), jnp.float32)], axis=0
@@ -303,19 +332,89 @@
     frame_grad[...] = (d0 + dt).astype(jnp.bfloat16)
 
 
-def score_and_grad(tau, total_pairs, feats, count):
-    vmem = pl.BlockSpec(memory_space=pltpu.VMEM)
+def finish_kernel(
+    tau,
+    total_pairs,
+    feats,
+    count,
+    pre_act,
+    w_second,
+    archive,
+    score,
+    grad_first,
+    grad_bias,
+    grad_second,
+    frame_grad,
+    d_pre,
+):
+    tile = feats.shape[1]
+
+    @pl.when(pl.program_id(0) == 0)
+    def _():
+        score_into(tau, total_pairs, feats, count, score, frame_grad)
+
+        @pl.loop(0, d_pre.shape[1] // tile)
+        def _(t):
+            part = pl.ds(pl.multiple_of(t * tile, tile), tile)
+            pre = pre_act[:, part].astype(jnp.float32)
+            low_exp = jnp.exp(jnp.minimum(pre, 0.0))
+            positive = pre > 0
+            hidden = jnp.where(positive, pre, low_exp - 1.0).astype(jnp.bfloat16)
+            back = lax.dot_general(
+                frame_grad[...],
+                w_second[part, :],
+                (NT, ((), ())),
+                preferred_element_type=jnp.float32,
+            )
+            grad = (back * jnp.where(positive, 1.0, low_exp)).astype(jnp.bfloat16)
+            d_pre[:, part] = grad
+            grad_bias[:, part] = jnp.sum(grad.astype(jnp.float32), axis=0, keepdims=True)
+            grad_second[part, :] = lax.dot_general(
+                hidden, frame_grad[...], (TN, ((), ())), preferred_element_type=jnp.float32
+            )
+
+    grad_first[...] = lax.dot_general(
+        archive[...], d_pre[...], (TN, ((), ())), preferred_element_type=jnp.float32
+    )
+
+
+def finish(tau, total_pairs, feats, count, pre_act, w_second, archive):
+    frames, feat = feats.shape
+    hid, field = w_second.shape[0], archive.shape[1]
+    tile = 256
+
+    def whole(shape):
+        return pl.BlockSpec(shape, lambda i: (0,) * len(shape))
+
     return pl.pallas_call(
-        functools.partial(score_kernel, tau, total_pairs),
+        functools.partial(finish_kernel, tau, total_pairs),
+        grid=(field // tile,),
         out_shape=(
             jax.ShapeDtypeStruct((8, 128), jnp.float32),
-            jax.ShapeDtypeStruct(feats.shape, jnp.bfloat16),
+            jax.ShapeDtypeStruct((field, hid), jnp.float32),
+            jax.ShapeDtypeStruct((1, hid), jnp.float32),
+            jax.ShapeDtypeStruct((hid, feat), jnp.float32),
         ),
-        in_specs=[vmem] * 2,
-        out_specs=(vmem, vmem),
+        in_specs=[
+            whole(feats.shape),
+            whole(count.shape),
+            whole(pre_act.shape),
+            whole(w_second.shape),
+            pl.BlockSpec((frames, tile), lambda i: (0, i)),
+        ],
+        out_specs=(
+            whole((8, 128)),
+            pl.BlockSpec((tile, hid), lambda i: (i, 0)),
+            whole((1, hid)),
+            whole((hid, feat)),
+        ),
+        scratch_shapes=[
+            pltpu.VMEM((frames, feat), jnp.bfloat16),
+            pltpu.VMEM((frames, hid), jnp.bfloat16),
+        ],
         compiler_params=pltpu.CompilerParams(vmem_limit_bytes=52 * MIB),
-        name="score",
-    )(feats, count)
+        name="finish",
+    )(feats, count, pre_act, w_second, archive)
 
 
 def per_device(n, archive, w_first, b_first, w_second, pair_table):
@@ -332,19 +431,10 @@
         (inst_index[:, None, None] == frame_ids[None]).astype(jnp.float32), axis=0
     )
     feats, pre_act, count = exchange(n, archive, w_first, b_first[None, :], w_second, count)
-    score, frame_grad = score_and_grad(tau, total_pairs, feats, count)
-    pre_act = pre_act.astype(jnp.float32)
-    hidden = elu(pre_act).astype(jnp.bfloat16)
-    slope = jnp.where(pre_act > 0, 1.0, jnp.exp(jnp.minimum(pre_act, 0.0)))
-    d_pre = (jnp.dot(frame_grad, w_second.T, preferred_element_type=jnp.float32) * slope).astype(
-        jnp.bfloat16
-    )
-    grad_second = jnp.dot(hidden.T, frame_grad, preferred_element_type=jnp.float32)
-    grad_bias = jnp.sum(d_pre.astype(jnp.float32), axis=0)
-    grad_first = lax.dot_general(
-        archive, d_pre, (((0,), (0,)), ((), ())), preferred_element_type=jnp.float32
-    )
-    return (score[0, :1], grad_first, grad_bias, grad_second)
+    score, grad_first, grad_bias, grad_second = finish(
+        tau, total_pairs, feats, count, pre_act, w_second, archive
+    )
+    return (score[0, :1], grad_first, grad_bias[0], grad_second)
 
 
 def solution(mesh):

time: 83.1 us -> 65.7 us (0.79)
  local copies, waits for them, and re-layouts: 11.7 us -> 2.24 us
  matrix products: 8.69 us -> 0 us
    unnamed x9 -> x6, local copies, waits for them, and re-layouts: 11.2 us -> 1.73 us
    dot_general x3 -> x0, matrix products: 8.69 us -> none  [the longest x1 5.61 us: per_device(): lax.dot_general(archive, d_pre, (((0,), (0,)), ((), ())), preferred_eleme...]
    pallas_call x1, Pallas kernels: 19.3 us -> 21.3 us  [finish(): pl.pallas_call(functools.partial(finish_kernel, tau, total_pairs), grid=(...]
    pallas_call x1, Pallas kernels: 41.4 us -> 39.9 us  [exchange(): pl.pallas_call(functools.partial(exchange_kernel, n), out_shape=(jax.Shap...]
where the time goes in v2:
time: 65.7 us; the launch traced here: 65.2 us
  Pallas kernels  61.2 us (93%)
  local copies, waits for them, and re-layouts  2.24 us (3%)
  other arithmetic  1.04 us (2%)
  between operations  0.66 us (1%)
    pallas_call x1, Pallas kernels, exchange(): pl.pallas_call(functools.partial(exchange_kernel, n), out_shape=(jax.Shap...  39.9 us
    pallas_call x1, Pallas kernels, finish(): pl.pallas_call(functools.partial(finish_kernel, tau, total_pairs), grid=(...  21.3 us
    unnamed x6, local copies, waits for them, and re-layouts  1.73 us

profile of v2, /device:TPU:27, one launch (start us, length us, event | category | flops | bytes accessed | tf_op | source)
XLA Modules:
  0.0 65.2 jit_solution(9035694811832763954)
XLA Ops:
  0.6 0.8 %add_bitcast_fusion = s32[128]{0:T(128)S(1)} fusion(s32[128,3]{0,1:T(4,128)} %param.9), kind=kLoop, calls=%fused_computation.3 | loop fusion | flops 256 | bytes 1536 | tf_op jit(solution)/shard_map/add | solution.py:425
  1.4 0.1 iota_add_fusion
  1.5 0.2 convert_reduce_fusion.count
  1.7 0.0 copy-start
  1.7 1.0 %copy-done = bf16[1024,256]{1,0:T(8,128)(2,1)S(1)} copy-done((bf16[1024,256]{1,0:T(8,128)(2,1)S(1)}, bf16[1024,256]{1,0:T(8,128)(2,1)}, u32[]{:S(2)}) %copy-start) | copy-done | bytes 524312
  2.7 0.0 copy-start.2
  2.7 0.7 %copy-done.2 = f32[1024]{0:T(1024)S(1)} copy-done((f32[1024]{0:T(1024)S(1)}, f32[1024]{0:T(1024)}, u32[]{:S(2)}) %copy-start.2) | copy-done | bytes 4120
  3.4 0.0 copy-start.1
  3.4 39.9 %exchange.1 = (bf16[512,256]{1,0:T(8,128)(2,1)S(1)}, bf16[512,1024]{1,0:T(8,128)(2,1)S(1)}, f32[8,128]{1,0:T(8,128)S(1)}) custom-call(bf16[512,2048]{1,0:T(8,128)(2,1)} %archive.3, bf16[2048,1024]{1,0:T(8,128)(2,1)} %w_first.1, f32[1,1024]{1,0:T(1,128)S(1)} %bitcast.5, bf16[1024,256]{1,0:T(8,128)(2,1)S(1)} %copy-done, f32[8,128]{1,0:T(8,128)S(1)} %convert_reduce_fusion.count), custom_call_target="tpu_custom_call" | custom-call | tf_op jit(solution)/shard_map/exchange/pallas_call | solution.py:228
  43.4 0.0 copy-done.1
  43.4 21.3 %finish.1 = (f32[8,128]{1,0:T(8,128)S(1)}, f32[2048,1024]{1,0:T(8,128)}, f32[1,1024]{1,0:T(1,128)}, f32[1024,256]{1,0:T(8,128)}) custom-call(bf16[512,256]{1,0:T(8,128)(2,1)S(1)} %get-tuple-element.11.feats, f32[8,128]{1,0:T(8,128)S(1)} %get-tuple-element.12.count, bf16[512,1024]{1,0:T(8,128)(2,1)S(1)} %get-tuple-element.13.pre_act, ...), custom_call_target="tpu_custom_call" | custom-call | tf_op jit(solution)/shard_map/finish/pallas_call | solution.py:389
  64.7 0.5 slice.11
  (1 shorter events, 0.0 us)
Async XLA Ops:
  1.7 1.0 %copy-start = (bf16[1024,256]{1,0:T(8,128)(2,1)S(1)}, bf16[1024,256]{1,0:T(8,128)(2,1)}, u32[]{:S(2)}) copy-start(bf16[1024,256]{1,0:T(8,128)(2,1)} %w_second.3) | copy-start | bytes 1572868
  2.7 0.7 %copy-start.2 = (f32[1024]{0:T(1024)S(1)}, f32[1024]{0:T(1024)}, u32[]{:S(2)}) copy-start(f32[1024]{0:T(1024)} %param.7) | copy-start | bytes 12292
  3.4 39.9 %copy-start.1 = (bf16[1024,256]{1,0:T(8,128)(2,1)S(1)}, bf16[1024,256]{1,0:T(8,128)(2,1)}, u32[]{:S(2)}) copy-start(bf16[1024,256]{1,0:T(8,128)(2,1)} %w_second.3) | copy-start | bytes 1572868

commit v3 on v2

--- a/solution.py
+++ b/solution.py
@@ -19,21 +19,31 @@
 
 def exchange_kernel(
     n,
+    tau,
+    total_pairs,
     archive,
     w_first,
+    b_hbm,
+    w_second_hbm,
+    index,
+    feats,
+    pre_all,
+    weight,
+    c00,
+    ctt,
+    c0t,
+    inv0,
+    invt,
+    info,
     b_first,
     w_second,
-    count,
-    feats,
-    pre_all,
-    count_out,
+    load_sem,
     out_half,
     in_half,
     own_half,
     send_buf,
     recv_buf,
-    count_in,
-    count_all,
+    index_all,
     pair_send,
     pair_recv,
     sum_send,
@@ -61,6 +71,12 @@
         other = lax.rem(chip + d, chips)
         return other, other * 2 + core
 
+    loads = [
+        pltpu.make_async_copy(b_hbm, b_first, load_sem.at[0]),
+        pltpu.make_async_copy(w_second_hbm, w_second, load_sem.at[1]),
+    ]
+    for load in loads:
+        load.start()
     barrier = pltpu.get_barrier_semaphore()
     pl.semaphore_signal(barrier, inc=1, device_id=to(partner), device_id_type=pl.DeviceIdType.MESH)
 
@@ -135,7 +151,10 @@
     def _(j):
         send_sum((1 - side) * side_chips + lax.rem(chip + j, side_chips))
 
-    cnt_copy = remote(count, count_in, cnt_send.at[chips], cnt_recv.at[chips], partner)
+    index_all[me] = jnp.broadcast_to(index[...], index_all.shape[1:])
+    cnt_copy = remote(
+        index_all.at[me], index_all.at[me], cnt_send.at[chips], cnt_recv.at[chips], partner
+    )
     cnt_copy.start()
     own_piece(side)
     near_copy.wait_recv()
@@ -145,12 +164,12 @@
         send_sum(side * side_chips + lax.rem(chip + j, side_chips))
 
     cnt_copy.wait()
-    count_all[chip] = count[...] + count_in[...]
+    for load in loads:
+        load.wait()
 
     def cnt_remote(d):
-        return remote(
-            count_all.at[chip], count_all.at[chip], cnt_send.at[d], cnt_recv.at[chip], peer_of(d)[1]
-        )
+        both = index_all.at[pl.ds(chip * 2, 2)]
+        return remote(both, both, cnt_send.at[d], cnt_recv.at[chip], peer_of(d)[1])
 
     @pl.loop(1, chips)
     def _(d):
@@ -205,11 +224,26 @@
     @pl.loop(1, chips)
     def _(d):
         other = peer_of(d)[0]
-        remote(count_all.at[other], count_all.at[other], cnt_send.at[d], cnt_recv.at[other], partner).wait_recv()
-
-    count_out[...] = jnp.sum(count_all[...], axis=0)
+        both = index_all.at[pl.ds(other * 2, 2)]
+        remote(both, both, cnt_send.at[d], cnt_recv.at[other], partner).wait_recv()
+
+    @pl.loop(0, frames // 128)
+    def _(t):
+        ids = t * 128 + lax.broadcasted_iota(jnp.int32, (128, index.shape[1]), 0)
+
+        def add(r, total):
+            return total + (index_all[r][0:1, :] == ids).astype(jnp.float32)
+
+        total = lax.fori_loop(0, n, add, jnp.zeros(ids.shape, jnp.float32))
+        weight[pl.ds(pl.multiple_of(t * 128, 128), 128), :] = jnp.sum(
+            total, axis=1, keepdims=True
+        )
+
+    feat_copy.wait()
+    start_inverse(tau, total_pairs, feats, weight, c00, ctt, c0t, inv0, invt, info)
+    refine(6, c00, ctt, inv0, invt, info)
     pre_copy = forward(pre_all, pre_send, pre_recv)
-    feat_copy.wait()
+    refine(3, c00, ctt, inv0, invt, info)
     pre_copy.wait()
 
     @pl.loop(1, chips)
@@ -220,28 +254,38 @@
         gather_remote(pre_all, pre_send, pre_recv, d).wait_send()
 
 
-def exchange(n, archive, w_first, b_first, w_second, count):
+def exchange(n, tau, total_pairs, archive, w_first, b_first, w_second, index):
     frames, hid, feat = archive.shape[0], w_first.shape[1], w_second.shape[1]
     half, chips, rows = frames // 2, n // 2, frames // n
     vmem = pl.BlockSpec(memory_space=pltpu.VMEM)
+    hbm = pl.BlockSpec(memory_space=pltpu.HBM)
     dma = pltpu.SemaphoreType.DMA
+    square = jax.ShapeDtypeStruct((feat, feat), jnp.float32)
     return pl.pallas_call(
-        functools.partial(exchange_kernel, n),
+        functools.partial(exchange_kernel, n, tau, total_pairs),
         out_shape=(
             jax.ShapeDtypeStruct((frames, feat), jnp.bfloat16),
             jax.ShapeDtypeStruct((frames, hid), jnp.bfloat16),
-            jax.ShapeDtypeStruct(count.shape, jnp.float32),
+            jax.ShapeDtypeStruct((frames, 1), jnp.float32),
+            square,
+            square,
+            square,
+            square,
+            square,
+            jax.ShapeDtypeStruct((8, 128), jnp.float32),
         ),
-        in_specs=[vmem] * 5,
-        out_specs=(vmem, vmem, vmem),
+        in_specs=[vmem, vmem, hbm, hbm, vmem],
+        out_specs=(vmem,) * 9,
         scratch_shapes=[
+            pltpu.VMEM(b_first.shape, jnp.float32),
+            pltpu.VMEM(w_second.shape, jnp.bfloat16),
+            dma((2,)),
             pltpu.VMEM((half, hid), jnp.float32),
             pltpu.VMEM((half, hid), jnp.float32),
             pltpu.VMEM((half, hid), jnp.float32),
             pltpu.VMEM((chips, rows, hid), jnp.bfloat16),
             pltpu.VMEM((chips, rows, hid), jnp.bfloat16),
-            pltpu.VMEM(count.shape, jnp.float32),
-            pltpu.VMEM((chips,) + count.shape, jnp.float32),
+            pltpu.VMEM((n, 8, index.shape[1]), jnp.int32),
             dma((2,)),
             dma((2,)),
             dma((chips,)),
@@ -254,10 +298,10 @@
             dma((chips + 1,)),
         ],
         compiler_params=pltpu.CompilerParams(
-            collective_id=0, has_side_effects=True, vmem_limit_bytes=52 * MIB
+            collective_id=0, has_side_effects=True, vmem_limit_bytes=40 * MIB
         ),
         name="exchange",
-    )(archive, w_first, b_first, w_second, count)
+    )(archive, w_first, b_first, w_second, index)
 
 
 def mm(a, b, dims=((1,), (0,))):
@@ -275,57 +319,90 @@
 NT = ((1,), (1,))
 
 
-def score_into(tau, total_pairs, feats, count, score, frame_grad):
-    frames, feat = feats.shape
-    columns = jnp.concatenate(
-        [count[...], jnp.zeros((128 - count.shape[0], 128), jnp.float32)], axis=0
-    ).T
-    n = jnp.concatenate([columns[:, i : i + 1] for i in range(frames // 128)], axis=0)
-    first = feats[...].astype(jnp.float32)
-    later = jnp.concatenate([first[tau:], first[:tau]], axis=0)
-    scale = 1.0 / total_pairs
-    x0 = first - jnp.sum(first * n, axis=0, keepdims=True) * scale
-    xt = later - jnp.sum(later * n, axis=0, keepdims=True) * scale
-    n = n * scale
-    x0n = x0 * n
-    xtn = xt * n
-    eye = (
+def identity(feat):
+    return (
         lax.broadcasted_iota(jnp.int32, (feat, feat), 0)
         == lax.broadcasted_iota(jnp.int32, (feat, feat), 1)
     ).astype(jnp.float32)
-    c00 = mm(x0n, x0, TN) + EPS * eye
-    ctt = mm(xtn, xt, TN) + EPS * eye
-    c0t = mm(x0n, xt, TN)
-    top0 = jnp.max(jnp.sum(jnp.abs(c00), axis=0, keepdims=True), axis=1, keepdims=True)
-    topt = jnp.max(jnp.sum(jnp.abs(ctt), axis=0, keepdims=True), axis=1, keepdims=True)
-    c00 = c00 / top0
-    ctt = ctt / topt
-    low = EPS / jnp.max(jnp.maximum(top0, topt))
-
-    def gain(low):
-        return 4.0 / jnp.square(1.0 + low)
-
-    a = gain(low) * ((1.0 + low) * eye - c00)
-    b = gain(low) * ((1.0 + low) * eye - ctt)
-
-    def step(carry):
-        low, a, b = carry
-        g = gain(low)
-        s = 1.0 + low
-        ra = s * eye - mm(c00, a)
-        rb = s * eye - mm(ctt, b)
-        return (jnp.minimum(g * low, 1.0), g * mm(a, ra), g * mm(b, rb))
-
-    _, a, b = lax.while_loop(lambda carry: carry[0] < 1.0 - 2e-6, step, (gain(low) * low, a, b))
-    a = a / top0
-    b = b / topt
-    u = mm(a, c0t)
-    v = mm(c0t, b)
+
+
+def centred_rows(tau, scale, feats, n):
+    first = feats[...].astype(jnp.float32)
+    later = jnp.concatenate([first[tau:], first[:tau]], axis=0)
+    x0 = first - jnp.sum(first * n, axis=0, keepdims=True) * scale
+    xt = later - jnp.sum(later * n, axis=0, keepdims=True) * scale
+    return x0, xt
+
+
+def gain(low):
+    return 4.0 / ((1.0 + low) * (1.0 + low))
+
+
+def start_inverse(tau, total_pairs, feats, weight, c00, ctt, c0t, inv0, invt, info):
+    n = weight[...]
+    scale = 1.0 / total_pairs
+    x0, xt = centred_rows(tau, scale, feats, n)
+    x0n = x0 * (n * scale)
+    eye = identity(feats.shape[1])
+    first = mm(x0n, x0, TN) + EPS * eye
+    c0t[...] = mm(x0n, xt, TN)
+    later = mm(xt * (n * scale), xt, TN) + EPS * eye
+    top0 = jnp.max(jnp.sum(jnp.abs(first), axis=0, keepdims=True), axis=1, keepdims=True)
+    topt = jnp.max(jnp.sum(jnp.abs(later), axis=0, keepdims=True), axis=1, keepdims=True)
+    first = first / top0
+    later = later / topt
+    low = EPS / jnp.maximum(top0, topt)
+    c00[...] = first
+    ctt[...] = later
+    inv0[...] = gain(low) * ((1.0 + low) * eye - first)
+    invt[...] = gain(low) * ((1.0 + low) * eye - later)
+    info[0:1, :] = jnp.broadcast_to(top0, (1, 128))
+    info[1:2, :] = jnp.broadcast_to(topt, (1, 128))
+    info[2:3, :] = jnp.broadcast_to(jnp.minimum(gain(low) * low, 1.0), (1, 128))
+
+
+def newton_step(c00, ctt, inv0, invt, low):
+    eye = identity(c00.shape[0])
+    a, b = inv0[...], invt[...]
+    ra = (1.0 + low) * eye - mm(c00[...], a)
+    rb = (1.0 + low) * eye - mm(ctt[...], b)
+    inv0[...] = gain(low) * mm(a, ra)
+    invt[...] = gain(low) * mm(b, rb)
+    return jnp.minimum(gain(low) * low, 1.0)
+
+
+def refine(steps, c00, ctt, inv0, invt, info):
+    @pl.loop(0, steps)
+    def _(_):
+        low = newton_step(c00, ctt, inv0, invt, info[2:3, 0:1])
+        info[2:3, :] = jnp.broadcast_to(low, (1, 128))
+
+
+def score_into(
+    tau, total_pairs, feats, weight, c00, ctt, c0t, start0, startt, info, score, frame_grad, inv0, invt
+):
+    inv0[...] = start0[...]
+    invt[...] = startt[...]
+    lax.while_loop(
+        lambda low: jnp.max(low) < 1.0 - 2e-6,
+        lambda low: newton_step(c00, ctt, inv0, invt, low),
+        info[2:3, 0:1],
+    )
+    a = inv0[...] / info[0:1, 0:1]
+    b = invt[...] / info[1:2, 0:1]
+    cross = c0t[...]
+    u = mm(a, cross)
+    v = mm(cross, b)
     k = mm(u, b)
     score[...] = jnp.broadcast_to(1.0 + jnp.sum(u * v), score.shape)
     g00 = -2.0 * mm(k, u, NT)
     gtt = -2.0 * mm(k, v, TN)
     k = 2.0 * k
+    n = weight[...]
+    scale = 1.0 / total_pairs
+    x0, xt = centred_rows(tau, scale, feats, n)
+    n = n * scale
+    frames = feats.shape[0]
     d0 = n * (mm(x0, g00) + mm(xt, k, NT))
     dt = n * (mm(x0, k) + mm(xt, gtt))
     dt = jnp.concatenate([dt[frames - tau :], dt[: frames - tau]], axis=0)
@@ -336,8 +413,14 @@
     tau,
     total_pairs,
     feats,
-    count,
     pre_act,
+    weight,
+    c00,
+    ctt,
+    c0t,
+    start0,
+    startt,
+    info,
     w_second,
     archive,
     score,
@@ -346,12 +429,29 @@
     grad_second,
     frame_grad,
     d_pre,
+    inv0,
+    invt,
 ):
     tile = feats.shape[1]
 
     @pl.when(pl.program_id(0) == 0)
     def _():
-        score_into(tau, total_pairs, feats, count, score, frame_grad)
+        score_into(
+            tau,
+            total_pairs,
+            feats,
+            weight,
+            c00,
+            ctt,
+            c0t,
+            start0,
+            startt,
+            info,
+            score,
+            frame_grad,
+            inv0,
+            invt,
+        )
 
         @pl.loop(0, d_pre.shape[1] // tile)
         def _(t):
@@ -378,8 +478,8 @@
     )
 
 
-def finish(tau, total_pairs, feats, count, pre_act, w_second, archive):
-    frames, feat = feats.shape
+def finish(tau, total_pairs, parts, w_second, archive):
+    frames, feat = parts[0].shape
     hid, field = w_second.shape[0], archive.shape[1]
     tile = 256
 
@@ -396,9 +496,7 @@
             jax.ShapeDtypeStruct((hid, feat), jnp.float32),
         ),
         in_specs=[
-            whole(feats.shape),
-            whole(count.shape),
-            whole(pre_act.shape),
+            *(whole(part.shape) for part in parts),
             whole(w_second.shape),
             pl.BlockSpec((frames, tile), lambda i: (0, i)),
         ],
@@ -411,10 +509,12 @@
         scratch_shapes=[
             pltpu.VMEM((frames, feat), jnp.bfloat16),
             pltpu.VMEM((frames, hid), jnp.bfloat16),
+            pltpu.VMEM((feat, feat), jnp.float32),
+            pltpu.VMEM((feat, feat), jnp.float32),
         ],
         compiler_params=pltpu.CompilerParams(vmem_limit_bytes=52 * MIB),
         name="finish",
-    )(feats, count, pre_act, w_second, archive)
+    )(*parts, w_second, archive)
 
 
 def per_device(n, archive, w_first, b_first, w_second, pair_table):
@@ -422,18 +522,10 @@
     steps_len = frames_total // TRAJS
     tau = frames_total // LAG_PARTS
     total_pairs = float(pair_table.shape[0] * n)
-    inst_index = pair_table[:, 2] * steps_len + pair_table[:, 0]
-    count_rows = max(8, frames_total // 128)
-    frame_ids = lax.broadcasted_iota(jnp.int32, (count_rows, 128), 0) * 128 + lax.broadcasted_iota(
-        jnp.int32, (count_rows, 128), 1
-    )
-    count = jnp.sum(
-        (inst_index[:, None, None] == frame_ids[None]).astype(jnp.float32), axis=0
-    )
-    feats, pre_act, count = exchange(n, archive, w_first, b_first[None, :], w_second, count)
-    score, grad_first, grad_bias, grad_second = finish(
-        tau, total_pairs, feats, count, pre_act, w_second, archive
-    )
+    columns = pair_table.T
+    index = columns[2:3] * steps_len + columns[0:1]
+    parts = exchange(n, tau, total_pairs, archive, w_first, b_first[None, :], w_second, index)
+    score, grad_first, grad_bias, grad_second = finish(tau, total_pairs, parts, w_second, archive)
     return (score[0, :1], grad_first, grad_bias[0], grad_second)
 
 

time: 65.7 us -> 60.9 us (0.927)
  the two profiles are of different devices: /device:TPU:27 before, /device:TPU:15 now
where the time goes in v3:
time: 60.9 us; the launch traced here: 60.5 us
  Pallas kernels  52.1 us (86%)
  local copies, waits for them, and re-layouts  6.98 us (11%)
  other arithmetic  0.76 us (1%)
  between operations  0.65 us (1%)
    pallas_call x1, Pallas kernels, exchange(): pl.pallas_call(functools.partial(exchange_kernel, n, tau, total_pairs), o...  39 us
    pallas_call x1, Pallas kernels, finish(): pl.pallas_call(functools.partial(finish_kernel, tau, total_pairs), grid=(...  13 us
    unnamed x10, local copies, waits for them, and re-layouts  6.47 us

profile of v3, /device:TPU:15, one launch (start us, length us, event | category | flops | bytes accessed | tf_op | source)
XLA Modules:
  0.0 60.5 jit_solution(7808024325423043288)
XLA Ops:
  0.6 0.8 %slice_add_fusion.index = s32[1,128]{1,0:T(1,128)S(1)} fusion(s32[3,128]{1,0:T(4,128)} %bitcast.6), kind=kLoop, calls=%fused_computation | loop fusion | flops 256 | bytes 1536 | tf_op jit(solution)/shard_map/add | solution.py:526
  1.4 0.0 copy-start
  1.4 1.6 %copy-done = bf16[512,2048]{1,0:T(8,128)(2,1)S(1)} copy-done((bf16[512,2048]{1,0:T(8,128)(2,1)S(1)}, bf16[512,2048]{1,0:T(8,128)(2,1)}, u32[]{:S(2)}) %copy-start) | copy-done | bytes 2097176
  3.0 0.0 copy-start.1
  3.0 2.2 %copy-done.1 = bf16[2048,1024]{1,0:T(8,128)(2,1)S(1)} copy-done((bf16[2048,1024]{1,0:T(8,128)(2,1)S(1)}, bf16[2048,1024]{1,0:T(8,128)(2,1)}, u32[]{:S(2)}) %copy-start.1) | copy-done | bytes 4194328
  5.2 0.0 copy-start.2
  5.2 1.0 %copy-done.2 = bf16[1024,256]{1,0:T(8,128)(2,1)S(1)} copy-done((bf16[1024,256]{1,0:T(8,128)(2,1)S(1)}, bf16[1024,256]{1,0:T(8,128)(2,1)}, u32[]{:S(2)}) %copy-start.2) | copy-done | bytes 524312
  6.2 0.0 copy-start.4
  6.2 0.7 %copy-done.4 = f32[1024]{0:T(1024)S(1)} copy-done((f32[1024]{0:T(1024)S(1)}, f32[1024]{0:T(1024)}, u32[]{:S(2)}) %copy-start.4) | copy-done | bytes 4120
  6.9 39.0 %exchange.1 = (bf16[512,256]{1,0:T(8,128)(2,1)S(1)}, bf16[512,1024]{1,0:T(8,128)(2,1)S(1)}, f32[512,1]{1,0:T(8,128)S(1)}, f32[256,256]{1,0:T(8,128)S(1)}, f32[25...) custom-call(bf16[512,2048]{1,0:T(8,128)(2,1)S(1)} %copy-done, ...), custom_call_target="tpu_custom_call" | custom-call | tf_op jit(solution)/shard_map/exchange/pallas_call | solution.py:264
  45.9 0.0 copy-start.3
  46.0 1.0 %copy-done.3 = bf16[512,1024]{1,0:T(8,128)(2,1)} copy-done((bf16[512,1024]{1,0:T(8,128)(2,1)}, bf16[512,1024]{1,0:T(8,128)(2,1)S(1)}, u32[]{:S(2)}) %copy-start.3) | copy-done | bytes 1048600
  46.9 13.0 %finish.1 = (f32[8,128]{1,0:T(8,128)S(1)}, f32[2048,1024]{1,0:T(8,128)}, f32[1,1024]{1,0:T(1,128)}, f32[1024,256]{1,0:T(8,128)}) custom-call(bf16[512,256]{1,0:T(8,128)(2,1)S(1)} %get-tuple-element.17.feats, bf16[512,1024]{1,0:T(8,128)(2,1)} %copy-done.3, f32[512,1]{1,0:T(8,128)S(1)} %get-tuple-element.19.weight, f32[256,256]{1,0:T(8,128)S(1)} %get-tuple-element.20.c00, ...), custom_call_target="tpu_custom_call" | custom-call | tf_op jit(solution)/shard_map/finish/pallas_call | solution.py:489
  60.0 0.5 slice.11
Async XLA Ops:
  1.4 1.6 %copy-start = (bf16[512,2048]{1,0:T(8,128)(2,1)S(1)}, bf16[512,2048]{1,0:T(8,128)(2,1)}, u32[]{:S(2)}) copy-start(bf16[512,2048]{1,0:T(8,128)(2,1)} %archive.3) | copy-start | bytes 6291460
  3.0 2.2 %copy-start.1 = (bf16[2048,1024]{1,0:T(8,128)(2,1)S(1)}, bf16[2048,1024]{1,0:T(8,128)(2,1)}, u32[]{:S(2)}) copy-start(bf16[2048,1024]{1,0:T(8,128)(2,1)} %w_first.1) | copy-start | bytes 12582916
  5.2 1.0 %copy-start.2 = (bf16[1024,256]{1,0:T(8,128)(2,1)S(1)}, bf16[1024,256]{1,0:T(8,128)(2,1)}, u32[]{:S(2)}) copy-start(bf16[1024,256]{1,0:T(8,128)(2,1)} %w_second.1) | copy-start | bytes 1572868
  6.2 0.7 %copy-start.4 = (f32[1024]{0:T(1024)S(1)}, f32[1024]{0:T(1024)}, u32[]{:S(2)}) copy-start(f32[1024]{0:T(1024)} %param.7) | copy-start | bytes 12292
  45.9 1.0 %copy-start.3 = (bf16[512,1024]{1,0:T(8,128)(2,1)}, bf16[512,1024]{1,0:T(8,128)(2,1)S(1)}, u32[]{:S(2)}) copy-start(bf16[512,1024]{1,0:T(8,128)(2,1)S(1)} %get-tuple-element.18.pre_act) | copy-start | bytes 3145732

commit v4 on v3

--- a/solution.py
+++ b/solution.py
@@ -21,8 +21,8 @@
     n,
     tau,
     total_pairs,
-    archive,
-    w_first,
+    archive_hbm,
+    w_first_hbm,
     b_hbm,
     w_second_hbm,
     index,
@@ -37,7 +37,11 @@
     info,
     b_first,
     w_second,
+    archive,
+    w_first,
     load_sem,
+    row_sem,
+    column_sem,
     out_half,
     in_half,
     own_half,
@@ -55,7 +59,7 @@
     pre_send,
     pre_recv,
 ):
-    frames, hid = archive.shape[0], w_first.shape[1]
+    frames, hid = archive_hbm.shape[0], w_first_hbm.shape[1]
     half = frames // 2
     chips = n // 2
     rows = frames // n
@@ -71,6 +75,25 @@
         other = lax.rem(chip + d, chips)
         return other, other * 2 + core
 
+    tile = 256
+    piece = half // 2
+    side_chips = chips // 2
+    side = chip // side_chips
+
+    def row_load(i):
+        start = (1 - core if i % 2 == 0 else core) * half + (1 - side if i < 2 else side) * piece
+        block = pl.ds(pl.multiple_of(start, 32), piece)
+        return pltpu.make_async_copy(archive_hbm.at[block], archive.at[block], row_sem.at[i])
+
+    def column_load(t):
+        cols = pl.ds(pl.multiple_of(t * tile, tile), tile)
+        return pltpu.make_async_copy(w_first_hbm.at[:, cols], w_first.at[:, cols], column_sem.at[t])
+
+    row_load(0).start()
+    for t in range(hid // tile):
+        column_load(t).start()
+    for i in range(1, 4):
+        row_load(i).start()
     loads = [
         pltpu.make_async_copy(b_hbm, b_first, load_sem.at[0]),
         pltpu.make_async_copy(w_second_hbm, w_second, load_sem.at[1]),
@@ -96,21 +119,17 @@
             device_id_type=pl.DeviceIdType.MESH,
         )
 
-    tile = 256
-
-    def matmul(row0, nrows, dst, dst0):
+    def matmul(row0, nrows, dst, dst0, first=False):
         @pl.loop(0, hid // tile)
         def _(t):
+            if first:
+                column_load(t).wait()
             cols = pl.ds(pl.multiple_of(t * tile, tile), tile)
             dst[pl.ds(dst0, nrows), cols] = jnp.dot(
                 archive[pl.ds(pl.multiple_of(row0, 32), nrows), :],
                 w_first[:, cols],
                 preferred_element_type=jnp.float32,
             )
-
-    piece = half // 2
-    side_chips = chips // 2
-    side = chip // side_chips
 
     def sum_remote(other):
         return remote(
@@ -128,7 +147,8 @@
 
     def partner_piece(which, index):
         start = pl.multiple_of(which * piece, 32)
-        matmul((1 - core) * half + start, piece, out_half, start)
+        row_load(2 * index).wait()
+        matmul((1 - core) * half + start, piece, out_half, start, index == 0)
         if index == 0:
             pl.semaphore_wait(barrier, chips)
         part = pl.ds(start, piece)
@@ -138,12 +158,13 @@
         copy.start()
         return copy
 
-    def own_piece(which):
+    def own_piece(which, index):
         start = pl.multiple_of(which * piece, 32)
+        row_load(2 * index + 1).wait()
         matmul(core * half + start, piece, own_half, start)
 
     far_copy = partner_piece(1 - side, 0)
-    own_piece(1 - side)
+    own_piece(1 - side, 0)
     near_copy = partner_piece(side, 1)
     far_copy.wait_recv()
 
@@ -156,7 +177,7 @@
         index_all.at[me], index_all.at[me], cnt_send.at[chips], cnt_recv.at[chips], partner
     )
     cnt_copy.start()
-    own_piece(side)
+    own_piece(side, 1)
     near_copy.wait_recv()
 
     @pl.loop(1, side_chips)
@@ -274,12 +295,16 @@
             square,
             jax.ShapeDtypeStruct((8, 128), jnp.float32),
         ),
-        in_specs=[vmem, vmem, hbm, hbm, vmem],
+        in_specs=[hbm, hbm, hbm, hbm, vmem],
         out_specs=(vmem,) * 9,
         scratch_shapes=[
             pltpu.VMEM(b_first.shape, jnp.float32),
             pltpu.VMEM(w_second.shape, jnp.bfloat16),
+            pltpu.VMEM(archive.shape, jnp.bfloat16),
+            pltpu.VMEM(w_first.shape, jnp.bfloat16),
             dma((2,)),
+            dma((4,)),
+            dma((hid // 256,)),
             pltpu.VMEM((half, hid), jnp.float32),
             pltpu.VMEM((half, hid), jnp.float32),
             pltpu.VMEM((half, hid), jnp.float32),
@@ -298,7 +323,7 @@
             dma((chips + 1,)),
         ],
         compiler_params=pltpu.CompilerParams(
-            collective_id=0, has_side_effects=True, vmem_limit_bytes=40 * MIB
+            collective_id=0, has_side_effects=True, vmem_limit_bytes=52 * MIB
         ),
         name="exchange",
     )(archive, w_first, b_first, w_second, index)

time: 60.9 us -> 59.1 us (0.970)
  the two profiles are of different devices: /device:TPU:15 before, /device:TPU:0 now
where the time goes in v4:
time: 59.1 us; the launch traced here: 58.7 us
  Pallas kernels  56.1 us (95%)
  local copies, waits for them, and re-layouts  1.2 us (2%)
  other arithmetic  0.76 us (1%)
  between operations  0.64 us (1%)
    pallas_call x1, Pallas kernels, exchange(): pl.pallas_call(functools.partial(exchange_kernel, n, tau, total_pairs), o...  43 us
    pallas_call x1, Pallas kernels, finish(): pl.pallas_call(functools.partial(finish_kernel, tau, total_pairs), grid=(...  13.1 us

profile of v4, /device:TPU:0, one launch (start us, length us, event | category | flops | bytes accessed | tf_op | source)
XLA Modules:
  0.0 58.7 jit_solution(5369117873738705017)
XLA Ops:
  0.6 0.8 %slice_add_fusion.index = s32[1,128]{1,0:T(1,128)S(1)} fusion(s32[3,128]{1,0:T(4,128)} %bitcast.6), kind=kLoop, calls=%fused_computation | loop fusion | flops 256 | bytes 1536 | tf_op jit(solution)/shard_map/add | solution.py:551
  1.4 0.0 copy-start
  1.4 0.7 %copy-done = f32[1024]{0:T(1024)S(1)} copy-done((f32[1024]{0:T(1024)S(1)}, f32[1024]{0:T(1024)}, u32[]{:S(2)}) %copy-start) | copy-done | bytes 4120
  2.1 43.0 %exchange.1 = (bf16[512,256]{1,0:T(8,128)(2,1)S(1)}, bf16[512,1024]{1,0:T(8,128)(2,1)}, f32[512,1]{1,0:T(8,128)S(1)}, f32[256,256]{1,0:T(8,128)S(1)}, f32[256,25...) custom-call(bf16[512,2048]{1,0:T(8,128)(2,1)} %archive.1, ...), custom_call_target="tpu_custom_call" | custom-call | tf_op jit(solution)/shard_map/exchange/pallas_call | solution.py:285
  45.1 13.1 %finish.1 = (f32[8,128]{1,0:T(8,128)S(1)}, f32[2048,1024]{1,0:T(8,128)}, f32[1,1024]{1,0:T(1,128)}, f32[1024,256]{1,0:T(8,128)}) custom-call(bf16[512,256]{1,0:T(8,128)(2,1)S(1)} %get-tuple-element.17.feats, bf16[512,1024]{1,0:T(8,128)(2,1)} %get-tuple-element.18.pre_act, f32[512,1]{1,0:T(8,128)S(1)} %get-tuple-element.19.weight, ...), custom_call_target="tpu_custom_call" | custom-call | tf_op jit(solution)/shard_map/finish/pallas_call | solution.py:514
  58.2 0.5 slice.11
Async XLA Ops:
  1.4 0.7 %copy-start = (f32[1024]{0:T(1024)S(1)}, f32[1024]{0:T(1024)}, u32[]{:S(2)}) copy-start(f32[1024]{0:T(1024)} %param.7) | copy-start | bytes 12292
